TPU v7x, 256 devices: a whole 4x4x8 slice. The times are simulated.
256 devices in a mesh: blk: 16 (over x_lo, z), dp: 16 (over x_hi, y, core).
Axes of the slice: x: 4 (x_hi: 2, x_lo: 2; x = x_hi * 2 + x_lo), y: 4, z: 8, core: 2. Of those that a mesh axis runs over, the one named last changes fastest.
Arguments:
- user_emb: bfloat16 [65536, 256], P(('blk', 'dp')), may hold values from -6 to 6
- pos_feat: bfloat16 [65536, 256], P(('blk', 'dp')), may hold values from -6 to 6
- pos_id: int32 [65536], P(('blk', 'dp')), may hold values from 0 to 4095
- neg_feat: bfloat16 [131072, 256], P(('blk', 'dp')), may hold values from -6 to 6
- neg_id: int32 [131072], P(('blk', 'dp')), may hold values from 0 to 4095
- neg_bucket: int32 [131072], P(('blk', 'dp')), may hold values from 0 to 1023
- logq_table: float32 [1024], replicated, may hold values from -4 to 0
- w_in: bfloat16 [256, 2048], replicated, may hold values from -0.375 to 0.375
- w_out: bfloat16 [2048, 256], replicated, may hold values from -0.125 to 0.125
Outputs:
- user_grad: float32 [65536, 256], P(('blk', 'dp'))
- w_in_grad: float32 [256, 2048], replicated
- w_out_grad: float32 [2048, 256], replicated
All inputs are finite; a program needn't handle non-finite values.
Results may differ from a plain program's by a relative error of at most 0.008.
Values may be sent and summed in bfloat16 or wider, within the bound.
No kernel may reach another device: no remote copies, remote signals or barrier semaphores. Data moves between devices by JAX's collectives and lax.ppermute only.
A program may use at most 128 MiB of HBM per device.

v0:
```python
import math
import jax
import jax.numpy as jnp
from jax import lax
from jax.sharding import PartitionSpec as P

score_gain = 2.0


def tower(feat, w_in, w_out):
    hidden = jnp.maximum(jnp.dot(feat, w_in, preferred_element_type=jnp.float32), 0.0).astype(
        jnp.bfloat16
    )
    emb = jnp.dot(hidden, w_out, preferred_element_type=jnp.float32).astype(jnp.bfloat16)
    return (hidden, emb)


def tower_grads(feat, hidden, emb_grad, w_out):
    back = jnp.dot(emb_grad, w_out.T, preferred_element_type=jnp.float32)
    back = jnp.where(hidden > 0, back, 0.0).astype(jnp.bfloat16)
    return (
        jnp.dot(feat.T, back, preferred_element_type=jnp.float32),
        jnp.dot(hidden.T, emb_grad, preferred_element_type=jnp.float32),
    )


def on_device(user_emb, pos_feat, pos_id, neg_feat, neg_id, neg_bucket, logq_table, w_in, w_out):
    scale = score_gain / math.sqrt(user_emb.shape[1])
    neg_hidden, neg_emb = tower(neg_feat, w_in, w_out)
    pos_hidden, pos_emb = tower(pos_feat, w_in, w_out)
    pos_score = scale * jnp.einsum(
        "ue,ue->u", user_emb, pos_emb, preferred_element_type=jnp.float32
    )
    pos_exp = jnp.exp(pos_score)
    all_emb, all_ids, all_buckets = (
        lax.all_gather(neg_emb, "blk", axis=0, tiled=True),
        lax.all_gather(neg_id, "blk", axis=0, tiled=True),
        lax.all_gather(neg_bucket, "blk", axis=0, tiled=True),
    )
    all_bias = jnp.take(logq_table, all_buckets)
    scores = (
        scale * jnp.dot(user_emb, all_emb.T, preferred_element_type=jnp.float32) - all_bias[None, :]
    )
    kept = jnp.where(all_ids[None, :] != pos_id[:, None], jnp.exp(scores), jnp.float32(0.0))
    total = pos_exp + jnp.sum(kept, axis=1)
    prob = (kept / total[:, None]).astype(jnp.bfloat16)
    pos_prob = pos_exp / total
    user_grad = scale * jnp.dot(prob, all_emb, preferred_element_type=jnp.float32) + scale * (
        pos_prob - 1.0
    )[:, None] * pos_emb.astype(jnp.float32)
    neg_grad = lax.psum_scatter(
        scale * jnp.dot(prob.T, user_emb, preferred_element_type=jnp.float32),
        "blk",
        scatter_dimension=0,
        tiled=True,
    ).astype(jnp.bfloat16)
    pos_grad = (scale * (pos_prob - 1.0)[:, None] * user_emb.astype(jnp.float32)).astype(
        jnp.bfloat16
    )
    neg_in, neg_out = tower_grads(neg_feat, neg_hidden, neg_grad, w_out)
    pos_in, pos_out = tower_grads(pos_feat, pos_hidden, pos_grad, w_out)
    w_in_grad, w_out_grad = lax.psum((neg_in + pos_in, neg_out + pos_out), ("blk", "dp"))
    return (user_grad, w_in_grad, w_out_grad)


def solution(mesh):
    return jax.shard_map(
        on_device,
        mesh=mesh,
        in_specs=(
            P(("blk", "dp"), None),
            P(("blk", "dp"), None),
            P(("blk", "dp")),
            P(("blk", "dp"), None),
            P(("blk", "dp")),
            P(("blk", "dp")),
            P(),
            P(),
            P(),
        ),
        out_specs=(P(("blk", "dp"), None), P(), P()),
        check_vma=False,
    )
```

profile of v0, /device:TPU:2, one launch (start us, length us, event | category | flops | bytes accessed | tf_op | source)
XLA Modules:
  0.0 515.9 jit_solution(11676487283757321345)
XLA Ops:
  7.2 0.0 copy-start
  7.2 0.0 all-gather.4.cloned.1.call-start
  7.2 1.1 copy-done
  8.4 1.7 maximum_convert_fusion
  10.1 1.3 copy-done.3
  11.4 2.6 convolution_convert_fusion
  14.0 0.0 all-gather.4.cloned.1.call-update
  14.1 0.0 reduce-scatter.2.cloned.1.call-start
  14.1 35.5 %all-gather.1 = s32[16,1,512]{2,1,0:T(1,128)S(1)} all-gather(s32[1,1,512]{2,1,0:T(1,128)S(1)} %bitcast.33), channel_id=1, replica_groups=mesh['blk'=16,'dp'=16] {'blk'}, dimensions={0}, use_global_device_ids=true | all-gather | bytes 34816 | tf_op jit(solution)/shard_map/all_gather | solution.py:38
  49.6 0.0 copy-start.12
  49.7 32.9 %gather_fusion = f32[8192]{0:T(1024)S(1)} fusion(f32[1024]{0:T(1024)S(1)} %copy-done.1, s32[8192]{0:T(1024)S(1)} %fusion.22), kind=kCustom, calls=%fused_computation | custom fusion | bytes 98304 | tf_op jit(solution)/shard_map/jit(_take)/gather | solution.py:40
  82.6 29.7 %all-gather = s32[16,1,512]{2,1,0:T(1,128)S(1)} all-gather(s32[1,1,512]{2,1,0:T(1,128)S(1)} %bitcast.34), channel_id=1, replica_groups=mesh['blk'=16,'dp'=16] {'blk'}, dimensions={0}, use_global_device_ids=true | all-gather | bytes 34816 | tf_op jit(solution)/shard_map/all_gather | solution.py:37
  112.3 0.4 fusion.5
  112.8 1.0 copy-done.4
  113.8 1.2 fusion.13
  114.9 6.7 %fusion.28 = (f32[256]{0:T(256)S(1)}, f32[256,8192]{0,1:T(8,128)S(1)}) fusion(f32[8192]{0:T(1024)S(1)} %and_select_fusion, bf16[8192,256]{1,0:T(8,128)(2,1)} %all-gather.4.cloned.1.call-done, bf16[256,256]{1,0:T(8,128)(2,1)S(1)} %copy-done.6, s32[256]{0:T(256)S(1)} %copy-done.13, s32[8192]{0:T(1024)S(1)} %bitcast.32), kind=kOutput, calls=%fused_computation.43 | convolution fusion | flops 1084227328 | bytes 12781568 | tf_op jit(solution)/shard_map/dot_general | solution.py:42
  121.6 0.8 divide_convert_fusion
  122.4 1.9 copy-done.2
  124.4 4.5 convolution_multiply_fusion
  128.8 0.0 reduce-scatter.2.cloned.1.call-update
  128.9 0.0 all-reduce.3.cloned.1.call-start
  128.9 1.8 fusion.18
  130.7 3.7 fusion.7
  134.4 93.3 %reduce-scatter.2.cloned.1.call-done = f32[512,256]{1,0:T(8,128)} async-done(((f32[8192,256]{1,0:T(8,128)}), f32[512,256]{1,0:T(8,128)}) %reduce-scatter.2.cloned.1.call-update) | async-done | bytes 524304 | tf_op jit(solution)/shard_map/reduce_scatter | solution.py:51
  227.7 3.7 convolution_add_fusion
  231.5 5.3 %fusion.4 = f32[256,2048]{0,1:T(8,128)} fusion(f32[2048,256]{1,0:T(8,128)} %fusion.7, bf16[512,256]{1,0:T(8,128)(2,1)S(1)} %copy-done.10, bf16[512,2048]{1,0:T(8,128)(2,1)} %copy-done.3, bf16[2048,256]{1,0:T(8,128)(2,1)} %param.17, f32[512,256]{1,0:T(8,128)} %reduce-scatter.2.cloned.1.call-done), kind=kOutput, calls=%fused_computation.13 | convolution fusion | flops 1077542912 | bytes 8126464 | tf_op jit(solution)/shard_map/dot_general | solution.py:22
  236.8 0.0 all-reduce.3.cloned.1.call-update
  236.8 0.9 copy-done.9
  237.7 5.5 %fusion.8 = f32[256,256]{1,0:T(8,128)} fusion(bf16[256,8192]{0,1:T(8,128)(2,1)} %copy-done.2, bf16[8192,256]{1,0:T(8,128)(2,1)} %all-gather.4.cloned.1.call-done, f32[256,256]{1,0:T(8,128)S(1)} %copy-done.9, f32[256]{0:T(256)S(1)} %get-tuple-element.14), kind=kOutput, calls=%fused_computation.20 | convolution fusion | flops 1073938432 | bytes 8913920 | tf_op jit(solution)/shard_map/dot_general | solution.py:48
  243.2 261.8 %all-reduce.3.cloned.1.call-done = (f32[256,2048]{0,1:T(8,128)}, f32[2048,256]{1,0:T(8,128)}) async-done(((f32[256,2048]{0,1:T(8,128)}, f32[2048,256]{1,0:T(8,128)}), (f32[256,2048]{0,1:T(8,128)}, f32[2048,256]{1,0:T(8,128)})) %all-reduce.3.cloned.1.call-update) | async-done | bytes 4194320 | tf_op jit(solution)/shard_map/psum | solution.py:62
  505.0 3.0 copy.14
  508.0 1.3 copy.22
  (25 shorter events, 0.1 us)
Async XLA Ops:
  7.2 1.2 copy-start
  7.2 6.9 %copy-start.11 = (s32[512]{0:T(512)S(1)}, s32[512]{0:T(512)}, u32[]{:S(2)}) copy-start(s32[512]{0:T(512)} %param.14) | copy-start | bytes 6148
  7.2 42.4 %copy-start.1 = (f32[1024]{0:T(1024)S(1)}, f32[1024]{0:T(1024)}, u32[]{:S(2)}) copy-start(f32[1024]{0:T(1024)} %param.15) | copy-start | bytes 12292
  7.2 107.7 %all-gather.4.cloned.1.call-start = ((), (), s32[]{:S(2)}) async-start(), calls=%async_computation.1 | async-start | bytes 4456448 | tf_op jit(solution)/shard_map/all_gather | solution.py:36
  10.1 1.3 copy-start.3
  14.1 213.6 %reduce-scatter.2.cloned.1.call-start = ((), (), s32[]{:S(2)}) async-start(), calls=%async_computation.2 | async-start | bytes 8912896 | tf_op jit(solution)/shard_map/reduce_scatter | solution.py:51
  49.6 32.9 %copy-start.12 = (s32[512]{0:T(512)S(1)}, s32[512]{0:T(512)}, u32[]{:S(2)}) copy-start(s32[512]{0:T(512)} %param.13) | copy-start | bytes 6148
  49.7 62.7 %copy-start.8 = (bf16[256,256]{1,0:T(8,128)(2,1)S(1)}, bf16[256,256]{1,0:T(8,128)(2,1)}, u32[]{:S(2)}) copy-start(bf16[256,256]{1,0:T(8,128)(2,1)} %param.10) | copy-start | bytes 393220
  49.7 64.1 %copy-start.5 = (bf16[2048,256]{1,0:T(8,128)(2,1)S(1)}, bf16[2048,256]{1,0:T(8,128)(2,1)}, u32[]{:S(2)}) copy-start(bf16[2048,256]{1,0:T(8,128)(2,1)} %param.17) | copy-start | bytes 3145732
  49.7 64.1 %copy-start.6 = (bf16[256,256]{1,0:T(8,128)(2,1)S(1)}, bf16[256,256]{1,0:T(8,128)(2,1)}, u32[]{:S(2)}) copy-start(bf16[256,256]{1,0:T(8,128)(2,1)} %param.9) | copy-start | bytes 393220
  82.6 32.3 %copy-start.13 = (s32[256]{0:T(256)S(1)}, s32[256]{0:T(256)}, u32[]{:S(2)}) copy-start(s32[256]{0:T(256)} %param.11) | copy-start | bytes 3076
  112.8 1.0 copy-start.4
  122.4 1.9 copy-start.2
  128.9 376.1 %all-reduce.3.cloned.1.call-start = ((), (), s32[]{:S(2)}) async-start(), calls=%async_computation.3 | async-start | bytes 8388608 | tf_op jit(solution)/shard_map/psum | solution.py:62
  134.4 97.1 %copy-start.10 = (bf16[512,256]{1,0:T(8,128)(2,1)S(1)}, bf16[512,256]{1,0:T(8,128)(2,1)}, u32[]{:S(2)}) copy-start(bf16[512,256]{1,0:T(8,128)(2,1)} %param.12) | copy-start | bytes 786436
  236.8 0.9 copy-start.9
  505.0 3.0 copy-start.7
Sparse Core Ops, SparseCore 0:
  14.2 78.2 all-gather.3
  129.0 98.6 reduce-scatter.1
  236.9 268.0 all-reduce.2
where the time goes:
time: 516 us
  waiting for transfers between devices  355 us (69%)
  blocking collectives  65.2 us (13%)
  local copies, waits for them, and re-layouts  43.6 us (8%)
  matrix products  37.1 us (7%)
  between operations  13.9 us (3%)
    psum x1, waiting for transfers between devices, on_device(): lax.psum((neg_in + pos_in, neg_out + pos_out), ('blk', 'dp'))  262 us
    reduce_scatter x1, waiting for transfers between devices, on_device(): lax.psum_scatter(scale * jnp.dot(prob.T, user_emb, preferred_element_type...  93.3 us
    all_gather x1, blocking collectives, on_device(): lax.all_gather(neg_bucket, 'blk', axis=0, tiled=True)  35.5 us
    gather x1, local copies, waits for them, and re-layouts, on_device(): all_bias = jnp.take(logq_table, all_buckets)  32.9 us
    all_gather x1, blocking collectives, on_device(): lax.all_gather(neg_id, 'blk', axis=0, tiled=True)  29.7 us
    unnamed x30, local copies, waits for them, and re-layouts  10.7 us
  transfers between devices with their start and end apart: 3, of which 2 were waited for; matrix products, arithmetic and copies ran while one was open for 9% of the time, Pallas kernels for 0%

commit v1 on v0

--- a/solution.py
+++ b/solution.py
@@ -34,7 +34,15 @@
     pos_exp = jnp.exp(pos_score)
     all_emb, all_ids, all_buckets = (
         lax.all_gather(neg_emb, "blk", axis=0, tiled=True),
-        lax.all_gather(neg_id, "blk", axis=0, tiled=True),
+        jnp.concatenate(
+            lax.all_to_all(
+                jnp.stack(lax.axis_size("blk") * [neg_id]),
+                axis_name="blk",
+                concat_axis=0,
+                split_axis=0,
+            ),
+            axis=0,
+        ),
         lax.all_gather(neg_bucket, "blk", axis=0, tiled=True),
     )
     all_bias = jnp.take(logq_table, all_buckets)

time: 516 us -> 495 us (0.959)
  blocking collectives: 65.2 us -> 32.4 us
  starting transfers between devices: 0.12 us -> 10.1 us
    all_gather x1 -> x0, blocking collectives: 29.7 us -> none  [on_device(): lax.all_gather(neg_id, 'blk', axis=0, tiled=True)]
    all_to_all x0 -> x1, starting transfers between devices: none -> 9.94 us  [on_device(): lax.all_to_all(jnp.stack(lax.axis_size('blk') * [neg_id]), axis_name='blk...]
  transfers between devices with their start and end apart: 3 -> 4, of which waited for: 2 -> 2; matrix products, arithmetic and copies ran while one was open for 9% -> 9% of each run, Pallas kernels for 0% -> 0%
where the time goes in v1:
time: 495 us; the launch traced here: 494 us
  waiting for transfers between devices  356 us (72%)
  local copies, waits for them, and re-layouts  44.2 us (9%)
  matrix products  37.1 us (7%)
  blocking collectives  32.4 us (7%)
  between operations  14 us (3%)
  starting transfers between devices  10.1 us (2%)
    psum x1, waiting for transfers between devices, on_device(): lax.psum((neg_in + pos_in, neg_out + pos_out), ('blk', 'dp'))  262 us
    reduce_scatter x1, waiting for transfers between devices, on_device(): lax.psum_scatter(scale * jnp.dot(prob.T, user_emb, preferred_element_type...  93.7 us
    gather x1, local copies, waits for them, and re-layouts, on_device(): all_bias = jnp.take(logq_table, all_buckets)  32.9 us
    all_gather x1, blocking collectives, on_device(): lax.all_gather(neg_bucket, 'blk', axis=0, tiled=True)  32.4 us
    unnamed x30, local copies, waits for them, and re-layouts  10.7 us
    all_to_all x1, starting transfers between devices, on_device(): lax.all_to_all(jnp.stack(lax.axis_size('blk') * [neg_id]), axis_name='blk...  9.94 us
  transfers between devices with their start and end apart: 4, of which 2 were waited for; matrix products, arithmetic and copies ran while one was open for 9% of the time, Pallas kernels for 0%

profile of v1, /device:TPU:2, one launch (start us, length us, event | category | flops | bytes accessed | tf_op | source)
XLA Modules:
  0.0 494.0 jit_solution(12519154885641123702)
XLA Ops:
  7.2 0.0 all-gather.3.cloned.1.call-start
  7.3 1.1 copy-done
  8.4 1.7 maximum_convert_fusion
  10.1 1.3 copy-done.3
  11.4 2.6 convolution_convert_fusion
  14.0 0.0 all-gather.3.cloned.1.call-update
  14.1 0.6 stack.2
  14.7 9.9 %all-to-all-start = ((s32[16,1,512]{2,1,0:T(1,128)}), s32[16,1,512]{2,1,0:T(1,128)S(1)}, u32[]{:S(2)}, u32[]{:S(2)}) async-start(s32[16,1,512]{2,1,0:T(1,128)} %stack.2), calls=%async_computation | async-start | bytes 65536 | tf_op jit(solution)/shard_map/all_to_all | solution.py:38
  24.6 0.0 reduce-scatter.2.cloned.1.call-start
  24.7 32.4 %all-gather = s32[16,1,512]{2,1,0:T(1,128)S(1)} all-gather(s32[1,1,512]{2,1,0:T(1,128)S(1)} %bitcast.32), channel_id=1, replica_groups=mesh['blk'=16,'dp'=16] {'blk'}, dimensions={0}, use_global_device_ids=true | all-gather | bytes 34816 | tf_op jit(solution)/shard_map/all_gather | solution.py:46
  57.2 32.9 %gather_fusion = f32[8192]{0:T(1024)S(1)} fusion(f32[1024]{0:T(1024)S(1)} %copy-done.1, s32[8192]{0:T(1024)S(1)} %fusion.22), kind=kCustom, calls=%fused_computation | custom fusion | bytes 98304 | tf_op jit(solution)/shard_map/jit(_take)/gather | solution.py:48
  90.1 0.4 fusion.5
  90.5 1.0 copy-done.4
  91.5 1.1 fusion.13
  92.7 0.0 all-gather.3.cloned.1.call-done
  92.7 6.7 %fusion.28 = (f32[256]{0:T(256)S(1)}, f32[256,8192]{0,1:T(8,128)S(1)}) fusion(f32[8192]{0:T(1024)S(1)} %and_select_fusion, bf16[8192,256]{1,0:T(8,128)(2,1)} %all-gather.3.cloned.1.call-done, bf16[256,256]{1,0:T(8,128)(2,1)S(1)} %copy-done.6, s32[256]{0:T(256)S(1)} %copy-done.13, s32[8192]{0:T(1024)S(1)} %bitcast.31), kind=kOutput, calls=%fused_computation.43 | convolution fusion | flops 1084227328 | bytes 12781568 | tf_op jit(solution)/shard_map/dot_general | solution.py:50
  99.4 0.8 divide_convert_fusion
  100.2 1.9 copy-done.2
  102.2 4.5 convolution_multiply_fusion
  106.6 0.0 reduce-scatter.2.cloned.1.call-update
  106.7 0.0 all-reduce.3.cloned.1.call-start
  106.7 1.8 fusion.18
  108.5 3.7 fusion.7
  112.2 93.7 %reduce-scatter.2.cloned.1.call-done = f32[512,256]{1,0:T(8,128)} async-done(((f32[8192,256]{1,0:T(8,128)}), f32[512,256]{1,0:T(8,128)}) %reduce-scatter.2.cloned.1.call-update) | async-done | bytes 524304 | tf_op jit(solution)/shard_map/reduce_scatter | solution.py:59
  205.9 3.8 convolution_add_fusion
  209.6 5.3 %fusion.4 = f32[256,2048]{0,1:T(8,128)} fusion(f32[2048,256]{1,0:T(8,128)} %fusion.7, bf16[512,256]{1,0:T(8,128)(2,1)S(1)} %copy-done.10, bf16[512,2048]{1,0:T(8,128)(2,1)} %copy-done.3, bf16[2048,256]{1,0:T(8,128)(2,1)} %param.17, f32[512,256]{1,0:T(8,128)} %reduce-scatter.2.cloned.1.call-done), kind=kOutput, calls=%fused_computation.13 | convolution fusion | flops 1077542912 | bytes 8126464 | tf_op jit(solution)/shard_map/dot_general | solution.py:22
  214.9 0.0 all-reduce.3.cloned.1.call-update
  215.0 0.9 copy-done.9
  215.9 5.4 %fusion.8 = f32[256,256]{1,0:T(8,128)} fusion(bf16[256,8192]{0,1:T(8,128)(2,1)} %copy-done.2, bf16[8192,256]{1,0:T(8,128)(2,1)} %all-gather.3.cloned.1.call-done, f32[256,256]{1,0:T(8,128)S(1)} %copy-done.9, f32[256]{0:T(256)S(1)} %get-tuple-element.14), kind=kOutput, calls=%fused_computation.20 | convolution fusion | flops 1073938432 | bytes 8913920 | tf_op jit(solution)/shard_map/dot_general | solution.py:56
  221.3 261.8 %all-reduce.3.cloned.1.call-done = (f32[256,2048]{0,1:T(8,128)}, f32[2048,256]{1,0:T(8,128)}) async-done(((f32[256,2048]{0,1:T(8,128)}, f32[2048,256]{1,0:T(8,128)}), (f32[256,2048]{0,1:T(8,128)}, f32[2048,256]{1,0:T(8,128)})) %all-reduce.3.cloned.1.call-update) | async-done | bytes 4194320 | tf_op jit(solution)/shard_map/psum | solution.py:70
  483.2 3.0 copy.14
  486.2 1.3 copy.22
  (27 shorter events, 0.1 us)
Async XLA Ops:
  7.2 1.2 copy-start
  7.2 6.9 %copy-start.11 = (s32[512]{0:T(512)S(1)}, s32[512]{0:T(512)}, u32[]{:S(2)}) copy-start(s32[512]{0:T(512)} %param.13) | copy-start | bytes 6148
  7.2 17.5 %copy-start.12 = (s32[512]{0:T(512)S(1)}, s32[512]{0:T(512)}, u32[]{:S(2)}) copy-start(s32[512]{0:T(512)} %param.14) | copy-start | bytes 6148
  7.2 49.9 %copy-start.1 = (f32[1024]{0:T(1024)S(1)}, f32[1024]{0:T(1024)}, u32[]{:S(2)}) copy-start(f32[1024]{0:T(1024)} %param.15) | copy-start | bytes 12292
  7.2 85.5 %all-gather.3.cloned.1.call-start = ((), (), s32[]{:S(2)}) async-start(), calls=%async_computation.2 | async-start | bytes 4456448 | tf_op jit(solution)/shard_map/all_gather | solution.py:36
  10.1 1.3 copy-start.3
  14.7 78.0 %all-to-all-start = ((s32[16,1,512]{2,1,0:T(1,128)}), s32[16,1,512]{2,1,0:T(1,128)S(1)}, u32[]{:S(2)}, u32[]{:S(2)}) async-start(s32[16,1,512]{2,1,0:T(1,128)} %stack.2), calls=%async_computation | async-start | bytes 65536 | tf_op jit(solution)/shard_map/all_to_all | solution.py:38
  24.6 181.2 %reduce-scatter.2.cloned.1.call-start = ((), (), s32[]{:S(2)}) async-start(), calls=%async_computation.3 | async-start | bytes 8912896 | tf_op jit(solution)/shard_map/reduce_scatter | solution.py:59
  57.1 32.9 %copy-start.8 = (bf16[256,256]{1,0:T(8,128)(2,1)S(1)}, bf16[256,256]{1,0:T(8,128)(2,1)}, u32[]{:S(2)}) copy-start(bf16[256,256]{1,0:T(8,128)(2,1)} %param.10) | copy-start | bytes 393220
  57.1 34.4 %copy-start.5 = (bf16[2048,256]{1,0:T(8,128)(2,1)S(1)}, bf16[2048,256]{1,0:T(8,128)(2,1)}, u32[]{:S(2)}) copy-start(bf16[2048,256]{1,0:T(8,128)(2,1)} %param.17) | copy-start | bytes 3145732
  57.1 34.4 %copy-start.6 = (bf16[256,256]{1,0:T(8,128)(2,1)S(1)}, bf16[256,256]{1,0:T(8,128)(2,1)}, u32[]{:S(2)}) copy-start(bf16[256,256]{1,0:T(8,128)(2,1)} %param.9) | copy-start | bytes 393220
  90.0 2.6 copy-start.13
  90.5 1.0 copy-start.4
  100.2 1.9 copy-start.2
  106.7 376.5 %all-reduce.3.cloned.1.call-start = ((), (), s32[]{:S(2)}) async-start(), calls=%async_computation.4 | async-start | bytes 8388608 | tf_op jit(solution)/shard_map/psum | solution.py:70
  112.2 97.4 %copy-start.10 = (bf16[512,256]{1,0:T(8,128)(2,1)S(1)}, bf16[512,256]{1,0:T(8,128)(2,1)}, u32[]{:S(2)}) copy-start(bf16[512,256]{1,0:T(8,128)(2,1)} %param.12) | copy-start | bytes 786436
  214.9 0.9 copy-start.9
  483.1 3.0 copy-start.7
Sparse Core Ops, SparseCore 0:
  14.2 78.3 all-gather.2
  106.8 99.0 reduce-scatter.1
  215.1 268.0 all-reduce.2
